TPU v7x, 32 devices: a whole 2x2x4 slice. The times are simulated.
32 devices in a mesh: tp: 4 (over x, core), ha: 2 (over y), wa: 4 (over z).
Axes of the slice: x: 2, y: 2, z: 4, core: 2. Of those that a mesh axis runs over, the one named last changes fastest.
Arguments:
- queries: bfloat16 [1, 4, 8, 128, 3072], P(None, 'ha', 'wa', None, 'tp'), may hold values from -128 to 128
- keys: bfloat16 [1, 4, 8, 128, 3072], P(None, 'ha', 'wa', None, 'tp'), may hold values from -4.5 to 4.5
- values: bfloat16 [1, 4, 8, 128, 3072], P(None, 'ha', 'wa', None, 'tp'), may hold values from -6 to 6
- grad_out: bfloat16 [1, 4, 8, 128, 3072], P(None, 'ha', 'wa', None, 'tp'), may hold values from -6 to 6
- out_proj: bfloat16 [3072, 3072], P(('ha', 'wa'), 'tp'), may hold values from -0.109375 to 0.109375
Outputs:
- grad_queries: bfloat16 [1, 4, 8, 128, 3072], P(None, 'ha', 'wa', None, 'tp')
- grad_keys: bfloat16 [1, 4, 8, 128, 3072], P(None, 'ha', 'wa', None, 'tp')
- grad_values: bfloat16 [1, 4, 8, 128, 3072], P(None, 'ha', 'wa', None, 'tp')
All inputs are finite; a program needn't handle non-finite values.
Results may differ from a plain program's by a relative error of at most 0.014.
Values may be sent and summed in bfloat16 or wider, within the bound.
A program may use at most 128 MiB of HBM per device.

v0:
```python
import functools

import jax
import jax.numpy as jnp
from jax import lax
from jax.experimental import pallas as pl
from jax.experimental.pallas import tpu as pltpu
from jax.sharding import PartitionSpec as P

HEAD = 128
MESH = pl.DeviceIdType.MESH
AROUND = ((0, -1), (0, 1), (-1, 0), (1, 0), (-1, -1), (-1, 1), (1, -1), (1, 1))
NT = (((1,), (1,)), ((), ()))
TN = (((0,), (0,)), ((), ()))


def inner_part(step, count):
    return {0: (1, count), -1: (1, 1), 1: (count, 1)}[step]


def outer_part(step, count):
    return {0: (1, count), -1: (0, 1), 1: (count + 1, 1)}[step]


def kernel(
    sizes,
    q_ref,
    k_ref,
    v_ref,
    g_ref,
    w_ref,
    dq_ref,
    dk_ref,
    dv_ref,
    k_ext,
    v_ext,
    g_all,
    w_all,
    ga,
    probs,
    totals,
    own,
    out_halo,
    *rest,
):
    in_halo = rest[:8]
    (
        local_sem,
        g_send,
        g_recv,
        kv_send,
        kv_recv,
        z_send,
        z_recv,
        y_send,
        y_recv,
        h_send,
        h_recv,
    ) = rest[8:]
    tp_n, ha_n, wa_n = sizes
    tp, ha, wa = (lax.axis_index(a) for a in ("tp", "ha", "wa"))
    rows, cols, tile, feat = k_ref.shape
    heads = feat // HEAD
    depth = w_ref.shape[0]
    f32, bf16 = jnp.float32, jnp.bfloat16

    def exists(step_r, step_c):
        r, c = ha + step_r, wa + step_c
        return (r >= 0) & (r < ha_n) & (c >= 0) & (c < wa_n)

    def at(step_r, step_c):
        return {"tp": tp, "ha": ha + step_r, "wa": wa + step_c}

    barrier = pltpu.get_barrier_semaphore()
    for k in range(1, tp_n):
        pl.semaphore_signal(
            barrier, inc=1, device_id={"tp": lax.rem(tp + k, tp_n), "ha": ha, "wa": wa}, device_id_type=MESH
        )
    for k in range(1, ha_n):
        pl.semaphore_signal(
            barrier, inc=1, device_id={"tp": tp, "ha": lax.rem(ha + k, ha_n), "wa": wa}, device_id_type=MESH
        )
    greeted = jnp.int32(tp_n - 1 + ha_n - 1)
    for step_r, step_c in AROUND:
        if step_c == 0:
            continue
        here = exists(step_r, step_c)
        greeted = greeted + here.astype(jnp.int32)

        @pl.when(here)
        def _():
            pl.semaphore_signal(barrier, inc=1, device_id=at(step_r, step_c), device_id_type=MESH)

    k_own = pltpu.make_async_copy(k_ref, k_ext.at[pl.ds(1, rows), pl.ds(1, cols)], local_sem.at[0])
    v_own = pltpu.make_async_copy(v_ref, v_ext.at[pl.ds(1, rows), pl.ds(1, cols)], local_sem.at[1])
    g_own = pltpu.make_async_copy(g_ref, g_all.at[tp], local_sem.at[2])
    w_rows = lambda block: pl.ds(pl.multiple_of(block * depth, 16), depth)
    w_own = pltpu.make_async_copy(w_ref, w_all.at[w_rows(ha * wa_n + wa)], local_sem.at[3])
    for copy in (k_own, v_own, g_own, w_own):
        copy.start()
    pl.semaphore_wait(barrier, greeted)

    def kv_copy(which, n):
        step_r, step_c = AROUND[n]
        src_r, len_r = inner_part(step_r, rows)
        src_c, len_c = inner_part(step_c, cols)
        dst_r, _ = outer_part(-step_r, rows)
        dst_c, _ = outer_part(-step_c, cols)
        src, dst = ((k_ref, k_ext), (v_ref, v_ext))[which]
        return pltpu.make_async_remote_copy(
            src_ref=src.at[pl.ds(src_r - 1, len_r), pl.ds(src_c - 1, len_c)],
            dst_ref=dst.at[pl.ds(dst_r, len_r), pl.ds(dst_c, len_c)],
            send_sem=kv_send.at[which, n],
            recv_sem=kv_recv.at[which, n],
            device_id=at(step_r, step_c),
            device_id_type=MESH,
        )

    def kv_arrival(which, n):
        step_r, step_c = AROUND[n]
        dst_r, len_r = outer_part(-step_r, rows)
        dst_c, len_c = outer_part(-step_c, cols)
        dst = (k_ext, v_ext)[which].at[pl.ds(dst_r, len_r), pl.ds(dst_c, len_c)]
        return pltpu.make_async_remote_copy(
            src_ref=dst,
            dst_ref=dst,
            send_sem=kv_send.at[which, n],
            recv_sem=kv_recv.at[which, n],
            device_id=at(-step_r, -step_c),
            device_id_type=MESH,
        )

    def each_way(do, sign=1):
        for n, (step_r, step_c) in enumerate(AROUND):

            @pl.when(exists(sign * step_r, sign * step_c))
            def _():
                do(n)

    each_way(lambda n: kv_copy(0, n).start())

    def g_copy(k):
        return pltpu.make_async_remote_copy(
            src_ref=g_ref,
            dst_ref=g_all.at[tp],
            send_sem=g_send.at[k - 1],
            recv_sem=g_recv.at[k - 1],
            device_id={"tp": lax.rem(tp + k, tp_n), "ha": ha, "wa": wa},
            device_id_type=MESH,
        )

    for k in range(1, tp_n):
        g_copy(k).start()

    def z_copy(way, step, source):
        where = w_all.at[w_rows(ha * wa_n + source)]
        return pltpu.make_async_remote_copy(
            src_ref=where,
            dst_ref=where,
            send_sem=z_send.at[way, step],
            recv_sem=z_recv.at[way, step],
            device_id={"tp": tp, "ha": ha, "wa": wa + (1, -1)[way]},
            device_id_type=MESH,
        )

    def y_copy(j, source, k, row):
        where = w_all.at[w_rows(row * wa_n + source)]
        return pltpu.make_async_remote_copy(
            src_ref=where,
            dst_ref=where,
            send_sem=y_send.at[j, k - 1],
            recv_sem=y_recv.at[j, k - 1],
            device_id={"tp": tp, "ha": lax.rem(ha + k, ha_n), "wa": wa},
            device_id_type=MESH,
        )

    def next_exists(way):
        return (wa + 1 < wa_n) if way == 0 else (wa >= 1)

    def source_of(way, step):
        source = wa - 1 - step if way == 0 else wa + 1 + step
        return source, ((source >= 0) if way == 0 else (source < wa_n))

    w_own.wait()
    for way in range(2):

        @pl.when(next_exists(way))
        def _():
            z_copy(way, 0, wa).start()

    for k in range(1, ha_n):
        y_copy(0, wa, k, ha).start()
    each_way(lambda n: kv_copy(1, n).start())

    def pass_on(step):
        for way in range(2):
            source, there = source_of(way, step)

            @pl.when(there)
            def _():
                z_copy(way, step, source).wait_recv()
                if step + 1 < wa_n - 1:

                    @pl.when(next_exists(way))
                    def _():
                        z_copy(way, step + 1, source).start()

                for k in range(1, ha_n):
                    y_copy(1 + way * (wa_n - 1) + step, source, k, ha).start()

    row_base, col_base = ha * rows, wa * cols
    scale = HEAD**-0.5

    def place(t):
        r, c = t // cols, t % cols
        start_r = jnp.clip(row_base + r - 1, 0, rows * ha_n - 3) - row_base + 1
        start_c = jnp.clip(col_base + c - 1, 0, cols * wa_n - 3) - col_base + 1
        return r, c, start_r, start_c

    def lanes(head):
        return pl.ds(pl.multiple_of(head * HEAD, HEAD), HEAD)

    def window(ext, start_r, start_c, head):
        return ext[pl.ds(start_r, 3), pl.ds(start_c, 3), :, lanes(head)].reshape(9 * tile, HEAD)

    def softmax_heads(first, last):
        @pl.loop(first, last)
        def _(head):
            for t in range(rows * cols):
                r, c, start_r, start_c = place(t)
                query = q_ref[r, c, :, lanes(head)]
                scores = lax.dot_general(
                    window(k_ext, start_r, start_c, head), query, NT, preferred_element_type=f32
                )
                scores = scores * scale
                expo = jnp.exp(scores - jnp.max(scores, axis=0, keepdims=True))
                inverse = 1.0 / jnp.sum(expo, axis=0, keepdims=True)
                probs[head, t] = (expo * inverse).astype(bf16)

    k_own.wait()
    each_way(lambda n: kv_arrival(0, n).wait_recv(), sign=-1)
    chunks = wa_n - 1
    for i in range(chunks):
        softmax_heads(i * heads // chunks, (i + 1) * heads // chunks)
        pass_on(i)

    g_own.wait()
    for k in range(1, tp_n):
        g_copy(k).wait_recv()
    v_own.wait()
    each_way(lambda n: kv_arrival(1, n).wait_recv(), sign=-1)
    for k in range(1, ha_n):
        row = lax.rem(ha + ha_n - k, ha_n)
        y_copy(0, wa, k, row).wait_recv()
        for way in range(2):
            for step in range(wa_n - 1):
                source, there = source_of(way, step)

                @pl.when(there)
                def _():
                    y_copy(1 + way * (wa_n - 1) + step, source, k, row).wait_recv()

    block = 256 if feat % 256 == 0 else 128

    @pl.loop(0, feat // block)
    def _(i):
        columns = pl.ds(pl.multiple_of(i * block, block), block)
        for half in range(2):
            m = rows * cols * tile // 2
            total = jnp.zeros((m, block), f32)
            for p in range(tp_n):
                total = total + jnp.dot(
                    g_all[p, half * m : (half + 1) * m, :],
                    w_all[p * feat : (p + 1) * feat, columns],
                    preferred_element_type=f32,
                )
            ga[half * m : (half + 1) * m, columns] = total.astype(bf16)

    def halo_copy(head, n):
        step_r, step_c = AROUND[n]
        src_r, len_r = outer_part(step_r, rows)
        src_c, len_c = outer_part(step_c, cols)
        return pltpu.make_async_remote_copy(
            src_ref=out_halo.at[head, :, pl.ds(src_r, len_r), pl.ds(src_c, len_c)],
            dst_ref=in_halo[n].at[head],
            send_sem=h_send.at[head, n],
            recv_sem=h_recv.at[head, n],
            device_id=at(step_r, step_c),
            device_id_type=MESH,
        )

    @pl.loop(0, heads)
    def _(head):
        totals[...] = jnp.zeros_like(totals)
        for t in range(rows * cols):
            r, c, start_r, start_c = place(t)
            grad = ga[t * tile : (t + 1) * tile, lanes(head)]
            prob = probs[head, t]
            grad_probs = lax.dot_general(
                window(v_ext, start_r, start_c, head), grad, NT, preferred_element_type=f32
            )
            weighted = prob.astype(f32) * grad_probs
            delta = jnp.sum(weighted, axis=0, keepdims=True)
            grad_scores = ((weighted - prob.astype(f32) * delta) * scale).astype(bf16)
            query = q_ref[r, c, :, lanes(head)]
            keys = window(k_ext, start_r, start_c, head)
            dq_ref[r, c, :, lanes(head)] = lax.dot_general(
                grad_scores, keys, TN, preferred_element_type=f32
            ).astype(bf16)
            shape = (3, 3, tile, HEAD)
            part = (pl.ds(start_r, 3), pl.ds(start_c, 3))
            grad_keys = jnp.dot(grad_scores, query, preferred_element_type=f32)
            totals[0, *part] += grad_keys.reshape(shape)
            grad_values = jnp.dot(prob, grad, preferred_element_type=f32)
            totals[1, *part] += grad_values.reshape(shape)
        own[head] = totals[:, 1 : rows + 1, 1 : cols + 1]
        out_halo[head] = totals[...].astype(bf16)
        each_way(lambda n: halo_copy(head, n).start())

    @pl.loop(0, heads)
    def _(head):
        for n, (step_r, step_c) in enumerate(AROUND):

            @pl.when(exists(-step_r, -step_c))
            def _():
                halo_copy(head, n).wait_recv()
                to_r, len_r = inner_part(-step_r, rows)
                to_c, len_c = inner_part(-step_c, cols)
                own[head, :, to_r - 1 : to_r - 1 + len_r, to_c - 1 : to_c - 1 + len_c] += in_halo[n][
                    head
                ].astype(f32)

        dk_ref[:, :, :, lanes(head)] = own[head, 0].astype(bf16)
        dv_ref[:, :, :, lanes(head)] = own[head, 1].astype(bf16)

    for which in range(2):
        each_way(lambda n: kv_copy(which, n).wait_send())
    for k in range(1, tp_n):
        g_copy(k).wait_send()
    for way in range(2):

        @pl.when(next_exists(way))
        def _():
            z_copy(way, 0, wa).wait_send()

        for step in range(wa_n - 1):
            source, there = source_of(way, step)

            if step + 1 < wa_n - 1:

                @pl.when(there & next_exists(way))
                def _():
                    z_copy(way, step + 1, source).wait_send()

            @pl.when(there)
            def _():
                for k in range(1, ha_n):
                    y_copy(1 + way * (wa_n - 1) + step, source, k, ha).wait_send()

    for k in range(1, ha_n):
        y_copy(0, wa, k, ha).wait_send()

    @pl.loop(0, heads)
    def _(head):
        each_way(lambda n: halo_copy(head, n).wait_send())


def local(queries, keys, values, grad_out, out_proj):
    frames, rows, cols, tile, feat = queries.shape
    heads = feat // HEAD
    tokens = rows * cols * tile
    tp_n, ha_n, wa_n = sizes = tuple(lax.axis_size(a) for a in ("tp", "ha", "wa"))
    blocks = queries.shape[1:]
    bf16, f32 = jnp.bfloat16, jnp.float32
    vmem, dma = pltpu.VMEM, pltpu.SemaphoreType.DMA
    length = lambda step, count: count if step == 0 else 1
    in_halo = [
        vmem((heads, 2, length(r, rows), length(c, cols), tile, HEAD), bf16) for r, c in AROUND
    ]
    whole = pl.BlockSpec(memory_space=pltpu.VMEM)
    anywhere = pl.BlockSpec(memory_space=pl.ANY)
    hops = wa_n - 1
    outs = pl.pallas_call(
        functools.partial(kernel, sizes),
        out_shape=[jax.ShapeDtypeStruct(blocks, bf16)] * 3,
        in_specs=[whole, anywhere, anywhere, anywhere, anywhere],
        out_specs=[whole] * 3,
        scratch_shapes=[
            vmem((rows + 2, cols + 2, tile, feat), bf16),
            vmem((rows + 2, cols + 2, tile, feat), bf16),
            vmem((tp_n, tokens, feat), bf16),
            vmem((out_proj.shape[0] * ha_n * wa_n, feat), bf16),
            vmem((tokens, feat), bf16),
            vmem((heads, rows * cols, 9 * tile, tile), bf16),
            vmem((2, rows + 2, cols + 2, tile, HEAD), f32),
            vmem((heads, 2, rows, cols, tile, HEAD), f32),
            vmem((heads, 2, rows + 2, cols + 2, tile, HEAD), bf16),
            *in_halo,
            dma((4,)),
            dma((tp_n - 1,)),
            dma((tp_n - 1,)),
            dma((2, 8)),
            dma((2, 8)),
            dma((2, hops)),
            dma((2, hops)),
            dma((1 + 2 * hops, ha_n - 1)),
            dma((1 + 2 * hops, ha_n - 1)),
            dma((heads, 8)),
            dma((heads, 8)),
        ],
        compiler_params=pltpu.CompilerParams(
            collective_id=0, has_side_effects=True, vmem_limit_bytes=60 * 2**20
        ),
    )(
        queries.reshape(blocks),
        keys.reshape(blocks),
        values.reshape(blocks),
        grad_out.reshape(tokens, feat),
        out_proj,
    )
    return tuple(out.reshape(queries.shape) for out in outs)


def solution(mesh):
    tiles = P(None, "ha", "wa", None, "tp")
    return jax.shard_map(
        local,
        mesh=mesh,
        in_specs=(tiles, tiles, tiles, tiles, P(("ha", "wa"), "tp")),
        out_specs=(tiles,) * 3,
        check_vma=False,
    )
```

profile of v0, /device:TPU:12, one launch (start us, length us, event | category | flops | bytes accessed | tf_op | source)
XLA Modules:
  0.0 138.1 jit_solution(1139648436820248563)
XLA Ops:
  0.6 133.0 %shard_map.76 = (bf16[2,2,128,768]{3,2,1,0:T(8,128)(2,1)}, bf16[2,2,128,768]{3,2,1,0:T(8,128)(2,1)}, bf16[2,2,128,768]{3,2,1,0:T(8,128)(2,1)}) custom-call(bf16[2,2,128,768]{3,2,1,0:T(8,128)(2,1)} %bitcast.7, bf16[2,2,128,768]{3,2,1,0:T(8,128)(2,1)} %bitcast.8, bf16[2,2,128,768]{3,2,1,0:T(8,128)(2,1)} %bitcast.9, bf16[512,768]{1,0:T(8,128)(2,1)} %bitcast.10, ...), custom_call_target="tpu_custom_call" | custom-call | tf_op jit(solution)/shard_map/pallas_call | solution.py:383
  133.7 0.0 copy-start.1
  133.7 2.1 %copy.11 = bf16[1,2,2,128,768]{4,3,2,1,0:T(8,128)(2,1)} copy(bf16[1,2,2,128,768]{4,3,2,1,0:T(8,128)(2,1)} %bitcast.13) | data formatting | bytes 1572864
  135.8 0.0 copy-done.1
  135.8 0.0 copy-start
  135.8 0.9 copy.12
  136.7 0.5 copy-done
  137.2 0.9 copy.13
Async XLA Ops:
  133.7 2.1 %copy-start.1 = (bf16[2,2,128,768]{3,2,1,0:T(8,128)(2,1)S(1)}, bf16[2,2,128,768]{3,2,1,0:T(8,128)(2,1)}, u32[]{:S(2)}) copy-start(bf16[2,2,128,768]{3,2,1,0:T(8,128)(2,1)} %get-tuple-element.7) | copy-start | bytes 2359300
  135.8 1.4 %copy-start = (bf16[2,2,128,768]{3,2,1,0:T(8,128)(2,1)S(1)}, bf16[2,2,128,768]{3,2,1,0:T(8,128)(2,1)}, u32[]{:S(2)}) copy-start(bf16[2,2,128,768]{3,2,1,0:T(8,128)(2,1)} %get-tuple-element.8) | copy-start | bytes 2359300
where the time goes:
time: 138 us
  Pallas kernels  133 us (96%)
  local copies, waits for them, and re-layouts  4.44 us (3%)
    pallas_call x1, Pallas kernels, local(): pl.pallas_call(functools.partial(kernel, sizes), out_shape=[jax.ShapeDtyp...  133 us
    unnamed x7, local copies, waits for them, and re-layouts  4.44 us

commit v1 on v0

--- a/solution.py
+++ b/solution.py
@@ -10,6 +10,7 @@
 HEAD = 128
 MESH = pl.DeviceIdType.MESH
 AROUND = ((0, -1), (0, 1), (-1, 0), (1, 0), (-1, -1), (-1, 1), (1, -1), (1, 1))
+COLUMNS, ROWS, CORNERS = (0, 1), (2, 3), (4, 5, 6, 7)
 NT = (((1,), (1,)), ((), ()))
 TN = (((0,), (0,)), ((), ()))
 
@@ -81,9 +82,8 @@
             barrier, inc=1, device_id={"tp": tp, "ha": lax.rem(ha + k, ha_n), "wa": wa}, device_id_type=MESH
         )
     greeted = jnp.int32(tp_n - 1 + ha_n - 1)
-    for step_r, step_c in AROUND:
-        if step_c == 0:
-            continue
+    for n in COLUMNS:
+        step_r, step_c = AROUND[n]
         here = exists(step_r, step_c)
         greeted = greeted + here.astype(jnp.int32)
 
@@ -102,23 +102,31 @@
 
     def kv_copy(which, n):
         step_r, step_c = AROUND[n]
-        src_r, len_r = inner_part(step_r, rows)
         src_c, len_c = inner_part(step_c, cols)
-        dst_r, _ = outer_part(-step_r, rows)
         dst_c, _ = outer_part(-step_c, cols)
         src, dst = ((k_ref, k_ext), (v_ref, v_ext))[which]
-        return pltpu.make_async_remote_copy(
-            src_ref=src.at[pl.ds(src_r - 1, len_r), pl.ds(src_c - 1, len_c)],
+        if step_r and step_c:
+            src_r, len_r = outer_part(step_r, rows)
+            dst_r = src_r
+            there = at(0, step_c)
+            src = dst.at[pl.ds(src_r, len_r), pl.ds(src_c, len_c)]
+        else:
+            src_r, len_r = inner_part(step_r, rows)
+            dst_r, _ = outer_part(-step_r, rows)
+            there = at(step_r, step_c)
+            src = src.at[pl.ds(src_r - 1, len_r), pl.ds(src_c - 1, len_c)]
+        return pltpu.make_async_remote_copy(
+            src_ref=src,
             dst_ref=dst.at[pl.ds(dst_r, len_r), pl.ds(dst_c, len_c)],
             send_sem=kv_send.at[which, n],
             recv_sem=kv_recv.at[which, n],
-            device_id=at(step_r, step_c),
+            device_id=there,
             device_id_type=MESH,
         )
 
     def kv_arrival(which, n):
         step_r, step_c = AROUND[n]
-        dst_r, len_r = outer_part(-step_r, rows)
+        dst_r, len_r = outer_part(step_r if step_c else -step_r, rows)
         dst_c, len_c = outer_part(-step_c, cols)
         dst = (k_ext, v_ext)[which].at[pl.ds(dst_r, len_r), pl.ds(dst_c, len_c)]
         return pltpu.make_async_remote_copy(
@@ -126,18 +134,27 @@
             dst_ref=dst,
             send_sem=kv_send.at[which, n],
             recv_sem=kv_recv.at[which, n],
-            device_id=at(-step_r, -step_c),
-            device_id_type=MESH,
-        )
-
-    def each_way(do, sign=1):
-        for n, (step_r, step_c) in enumerate(AROUND):
-
-            @pl.when(exists(sign * step_r, sign * step_c))
+            device_id=at(0 if step_c else -step_r, -step_c),
+            device_id_type=MESH,
+        )
+
+    def outgoing(do, ways):
+        for n in ways:
+            step_r, step_c = AROUND[n]
+
+            @pl.when(exists(step_r, step_c))
             def _():
                 do(n)
 
-    each_way(lambda n: kv_copy(0, n).start())
+    def incoming(do, ways):
+        for n in ways:
+            step_r, step_c = AROUND[n]
+
+            @pl.when(exists(step_r if step_c else -step_r, -step_c))
+            def _():
+                do(n)
+
+    outgoing(lambda n: kv_copy(0, n).start(), ROWS + COLUMNS)
 
     def g_copy(k):
         return pltpu.make_async_remote_copy(
@@ -190,7 +207,7 @@
 
     for k in range(1, ha_n):
         y_copy(0, wa, k, ha).start()
-    each_way(lambda n: kv_copy(1, n).start())
+    outgoing(lambda n: kv_copy(1, n).start(), ROWS + COLUMNS)
 
     def pass_on(step):
         for way in range(2):
@@ -237,18 +254,23 @@
                 inverse = 1.0 / jnp.sum(expo, axis=0, keepdims=True)
                 probs[head, t] = (expo * inverse).astype(bf16)
 
+    incoming(lambda n: kv_arrival(0, n).wait_recv(), ROWS)
+    outgoing(lambda n: kv_copy(0, n).start(), CORNERS)
     k_own.wait()
-    each_way(lambda n: kv_arrival(0, n).wait_recv(), sign=-1)
+    incoming(lambda n: kv_arrival(0, n).wait_recv(), COLUMNS + CORNERS)
     chunks = wa_n - 1
     for i in range(chunks):
         softmax_heads(i * heads // chunks, (i + 1) * heads // chunks)
         pass_on(i)
+        if i == 0:
+            incoming(lambda n: kv_arrival(1, n).wait_recv(), ROWS)
+            outgoing(lambda n: kv_copy(1, n).start(), CORNERS)
 
     g_own.wait()
     for k in range(1, tp_n):
         g_copy(k).wait_recv()
     v_own.wait()
-    each_way(lambda n: kv_arrival(1, n).wait_recv(), sign=-1)
+    incoming(lambda n: kv_arrival(1, n).wait_recv(), COLUMNS + CORNERS)
     for k in range(1, ha_n):
         row = lax.rem(ha + ha_n - k, ha_n)
         y_copy(0, wa, k, row).wait_recv()
@@ -285,9 +307,21 @@
             dst_ref=in_halo[n].at[head],
             send_sem=h_send.at[head, n],
             recv_sem=h_recv.at[head, n],
-            device_id=at(step_r, step_c),
-            device_id_type=MESH,
-        )
+            device_id=at(0 if step_c else step_r, step_c),
+            device_id_type=MESH,
+        )
+
+    def send_rows(head):
+        def add(n):
+            step_r, step_c = AROUND[n]
+            halo_copy(head, n).wait_recv()
+            r, _ = outer_part(step_r, rows)
+            c, _ = inner_part(-step_c, cols)
+            total = out_halo[head, :, r, c].astype(f32) + in_halo[n][head, :, 0, 0].astype(f32)
+            out_halo[head, :, r, c] = total.astype(bf16)
+
+        incoming(add, CORNERS)
+        outgoing(lambda n: halo_copy(head, n).start(), ROWS)
 
     @pl.loop(0, heads)
     def _(head):
@@ -315,11 +349,18 @@
             totals[1, *part] += grad_values.reshape(shape)
         own[head] = totals[:, 1 : rows + 1, 1 : cols + 1]
         out_halo[head] = totals[...].astype(bf16)
-        each_way(lambda n: halo_copy(head, n).start())
+        outgoing(lambda n: halo_copy(head, n).start(), COLUMNS + CORNERS)
+
+        @pl.when(head > 0)
+        def _():
+            send_rows(head - 1)
+
+    send_rows(heads - 1)
 
     @pl.loop(0, heads)
     def _(head):
-        for n, (step_r, step_c) in enumerate(AROUND):
+        for n in COLUMNS + ROWS:
+            step_r, step_c = AROUND[n]
 
             @pl.when(exists(-step_r, -step_c))
             def _():
@@ -334,7 +375,7 @@
         dv_ref[:, :, :, lanes(head)] = own[head, 1].astype(bf16)
 
     for which in range(2):
-        each_way(lambda n: kv_copy(which, n).wait_send())
+        outgoing(lambda n: kv_copy(which, n).wait_send(), range(8))
     for k in range(1, tp_n):
         g_copy(k).wait_send()
     for way in range(2):
@@ -362,7 +403,7 @@
 
     @pl.loop(0, heads)
     def _(head):
-        each_way(lambda n: halo_copy(head, n).wait_send())
+        outgoing(lambda n: halo_copy(head, n).wait_send(), range(8))
 
 
 def local(queries, keys, values, grad_out, out_proj):

time: 138 us -> 134 us (0.971)
  the two profiles are of different devices: /device:TPU:12 before, /device:TPU:0 now
where the time goes in v1:
time: 134 us
  Pallas kernels  129 us (96%)
  local copies, waits for them, and re-layouts  4.44 us (3%)
    pallas_call x1, Pallas kernels, local(): pl.pallas_call(functools.partial(kernel, sizes), out_shape=[jax.ShapeDtyp...  129 us
    unnamed x7, local copies, waits for them, and re-layouts  4.44 us

profile of v1, /device:TPU:0, one launch (start us, length us, event | category | flops | bytes accessed | tf_op | source)
XLA Modules:
  0.0 133.8 jit_solution(8422992858302201925)
XLA Ops:
  0.6 128.7 %shard_map.76 = (bf16[2,2,128,768]{3,2,1,0:T(8,128)(2,1)}, bf16[2,2,128,768]{3,2,1,0:T(8,128)(2,1)}, bf16[2,2,128,768]{3,2,1,0:T(8,128)(2,1)}) custom-call(bf16[2,2,128,768]{3,2,1,0:T(8,128)(2,1)} %bitcast.7, bf16[2,2,128,768]{3,2,1,0:T(8,128)(2,1)} %bitcast.8, bf16[2,2,128,768]{3,2,1,0:T(8,128)(2,1)} %bitcast.9, bf16[512,768]{1,0:T(8,128)(2,1)} %bitcast.10, ...), custom_call_target="tpu_custom_call" | custom-call | tf_op jit(solution)/shard_map/pallas_call | solution.py:424
  129.4 0.0 copy-start.1
  129.4 2.1 %copy.11 = bf16[1,2,2,128,768]{4,3,2,1,0:T(8,128)(2,1)} copy(bf16[1,2,2,128,768]{4,3,2,1,0:T(8,128)(2,1)} %bitcast.13) | data formatting | bytes 1572864
  131.5 0.0 copy-done.1
  131.5 0.0 copy-start
  131.5 0.9 copy.12
  132.4 0.5 copy-done
  132.9 0.9 copy.13
Async XLA Ops:
  129.4 2.1 %copy-start.1 = (bf16[2,2,128,768]{3,2,1,0:T(8,128)(2,1)S(1)}, bf16[2,2,128,768]{3,2,1,0:T(8,128)(2,1)}, u32[]{:S(2)}) copy-start(bf16[2,2,128,768]{3,2,1,0:T(8,128)(2,1)} %get-tuple-element.7) | copy-start | bytes 2359300
  131.5 1.4 %copy-start = (bf16[2,2,128,768]{3,2,1,0:T(8,128)(2,1)S(1)}, bf16[2,2,128,768]{3,2,1,0:T(8,128)(2,1)}, u32[]{:S(2)}) copy-start(bf16[2,2,128,768]{3,2,1,0:T(8,128)(2,1)} %get-tuple-element.8) | copy-start | bytes 2359300

commit v2 on v1

--- a/solution.py
+++ b/solution.py
@@ -154,7 +154,6 @@
             def _():
                 do(n)
 
-    outgoing(lambda n: kv_copy(0, n).start(), ROWS + COLUMNS)
 
     def g_copy(k):
         return pltpu.make_async_remote_copy(
@@ -166,9 +165,6 @@
             device_id_type=MESH,
         )
 
-    for k in range(1, tp_n):
-        g_copy(k).start()
-
     def z_copy(way, step, source):
         where = w_all.at[w_rows(ha * wa_n + source)]
         return pltpu.make_async_remote_copy(
@@ -207,6 +203,9 @@
 
     for k in range(1, ha_n):
         y_copy(0, wa, k, ha).start()
+    outgoing(lambda n: kv_copy(0, n).start(), ROWS + COLUMNS)
+    for k in range(1, tp_n):
+        g_copy(k).start()
     outgoing(lambda n: kv_copy(1, n).start(), ROWS + COLUMNS)
 
     def pass_on(step):
@@ -254,6 +253,7 @@
                 inverse = 1.0 / jnp.sum(expo, axis=0, keepdims=True)
                 probs[head, t] = (expo * inverse).astype(bf16)
 
+    pass_on(0)
     incoming(lambda n: kv_arrival(0, n).wait_recv(), ROWS)
     outgoing(lambda n: kv_copy(0, n).start(), CORNERS)
     k_own.wait()
@@ -261,7 +261,8 @@
     chunks = wa_n - 1
     for i in range(chunks):
         softmax_heads(i * heads // chunks, (i + 1) * heads // chunks)
-        pass_on(i)
+        if i + 1 < chunks:
+            pass_on(i + 1)
         if i == 0:
             incoming(lambda n: kv_arrival(1, n).wait_recv(), ROWS)
             outgoing(lambda n: kv_copy(1, n).start(), CORNERS)

time: 134 us -> 128 us (0.955)
  Pallas kernels: 129 us -> 123 us
    pallas_call x1, Pallas kernels: 129 us -> 123 us  [local(): pl.pallas_call(functools.partial(kernel, sizes), out_shape=[jax.ShapeDtyp...]
where the time goes in v2:
time: 128 us
  Pallas kernels  123 us (96%)
  local copies, waits for them, and re-layouts  4.44 us (3%)
    pallas_call x1, Pallas kernels, local(): pl.pallas_call(functools.partial(kernel, sizes), out_shape=[jax.ShapeDtyp...  123 us
    unnamed x7, local copies, waits for them, and re-layouts  4.44 us

profile of v2, /device:TPU:0, one launch (start us, length us, event | category | flops | bytes accessed | tf_op | source)
XLA Modules:
  0.0 127.6 jit_solution(12772679028554567594)
XLA Ops:
  0.6 122.5 %shard_map.76 = (bf16[2,2,128,768]{3,2,1,0:T(8,128)(2,1)}, bf16[2,2,128,768]{3,2,1,0:T(8,128)(2,1)}, bf16[2,2,128,768]{3,2,1,0:T(8,128)(2,1)}) custom-call(bf16[2,2,128,768]{3,2,1,0:T(8,128)(2,1)} %bitcast.7, bf16[2,2,128,768]{3,2,1,0:T(8,128)(2,1)} %bitcast.8, bf16[2,2,128,768]{3,2,1,0:T(8,128)(2,1)} %bitcast.9, bf16[512,768]{1,0:T(8,128)(2,1)} %bitcast.10, ...), custom_call_target="tpu_custom_call" | custom-call | tf_op jit(solution)/shard_map/pallas_call | solution.py:425
  123.2 0.0 copy-start.1
  123.2 2.1 %copy.11 = bf16[1,2,2,128,768]{4,3,2,1,0:T(8,128)(2,1)} copy(bf16[1,2,2,128,768]{4,3,2,1,0:T(8,128)(2,1)} %bitcast.13) | data formatting | bytes 1572864
  125.3 0.0 copy-done.1
  125.3 0.0 copy-start
  125.3 0.9 copy.12
  126.2 0.5 copy-done
  126.7 0.9 copy.13
Async XLA Ops:
  123.2 2.1 %copy-start.1 = (bf16[2,2,128,768]{3,2,1,0:T(8,128)(2,1)S(1)}, bf16[2,2,128,768]{3,2,1,0:T(8,128)(2,1)}, u32[]{:S(2)}) copy-start(bf16[2,2,128,768]{3,2,1,0:T(8,128)(2,1)} %get-tuple-element.7) | copy-start | bytes 2359300
  125.3 1.4 %copy-start = (bf16[2,2,128,768]{3,2,1,0:T(8,128)(2,1)S(1)}, bf16[2,2,128,768]{3,2,1,0:T(8,128)(2,1)}, u32[]{:S(2)}) copy-start(bf16[2,2,128,768]{3,2,1,0:T(8,128)(2,1)} %get-tuple-element.8) | copy-start | bytes 2359300
